TPU v7x, 256 devices: a whole 4x4x8 slice. The times are simulated.
256 devices in a mesh: band: 64 (over z, x_lo, y), pc: 4 (over x_hi, core).
Axes of the slice: x: 4 (x_hi: 2, x_lo: 2; x = x_hi * 2 + x_lo), y: 4, z: 8, core: 2. Of those that a mesh axis runs over, the one named last changes fastest.
Arguments:
- planes: bfloat16 [3, 256, 256, 256], P(None, 'band', 'pc'), may hold values from -15 to 15
- cotangent: bfloat16 [3, 256, 256, 256], P(None, 'band', 'pc'), may hold values from -6 to 6
- conv_weight: bfloat16 [9, 256, 256], P(None, 'pc'), may hold values from -0.125 to 0.125
- context_gain: bfloat16 [256], P('pc'), may hold values from 0.5 to 1.5
- step_index: int32 [1], replicated, may hold values from 0 to 999
Outputs:
- block_out: bfloat16 [3, 256, 256, 256], P(None, 'band', 'pc')
- input_grad: bfloat16 [3, 256, 256, 256], P(None, 'band', 'pc')
- weight_grad: float32 [9, 256, 256], P(None, 'pc', 'band')
All inputs are finite; a program needn't handle non-finite values.
Results may differ from a plain program's by a relative error of at most 0.0027.
The roundings to bfloat16 on the way count: a program that leaves them out, or rounds other values in their place, can miss the bound.
Values may be sent and summed in bfloat16 or wider, within the bound.
A program may use at most 64 MiB of HBM per device.

v0:
```python
import math
import jax
import jax.numpy as jnp
from jax import lax
from jax.sharding import PartitionSpec as P

C = 256


def with_halo(block, sides, width):
    for axis, dim in sides:
        count = lax.axis_size(axis)
        forward = [(i, i + 1) for i in range(count - 1)]
        backward = [(target, source) for source, target in forward]
        low = lax.ppermute(
            lax.slice_in_dim(block, block.shape[dim] - width, None, axis=dim), axis, forward
        )
        high = lax.ppermute(lax.slice_in_dim(block, 0, width, axis=dim), axis, backward)
        block = jnp.concatenate([low, block, high], axis=dim)
    return block


def time_embed(step_index, channel_ids, channels):
    moment = step_index[0].astype(jnp.float32)
    frequency = jnp.exp(
        -math.log(10000.0) * (2 * (channel_ids // 2)).astype(jnp.float32) / channels
    )
    phase = moment * frequency
    return jnp.where(channel_ids % 2 == 0, jnp.sin(phase), jnp.cos(phase))


def pooled(values):
    col_sums = jnp.sum(values, axis=1)
    row_sums = jnp.sum(values, axis=3)
    totals = lax.psum(col_sums, "band")
    row_sums_all = lax.all_gather(row_sums[2], "band", axis=0, tiled=True)
    return (totals, row_sums, row_sums_all)


def context(values, first_row, side_cells):
    totals, row_sums, row_sums_all = pooled(values)
    row_count = values.shape[1]
    own_columns = lax.dynamic_slice_in_dim(totals[0], first_row, row_count, 1)
    plane_one = row_sums[1][:, :, None] + jnp.transpose(row_sums_all)[None]
    plane_two = row_sums[0][:, :, None] + totals[2][None]
    plane_three = jnp.transpose(own_columns)[:, :, None] + totals[1][None]
    return jnp.stack([plane_one, plane_two, plane_three]) / side_cells


def convolve(values, weight, row_count, col_count):
    total = jnp.zeros((3, row_count, weight.shape[1], col_count), jnp.float32)
    for row_tap in range(3):
        for col_tap in range(3):
            window = values[:, row_tap : row_tap + row_count, :, col_tap : col_tap + col_count]
            total = total + jnp.einsum(
                "oc,kicj->kioj",
                weight[3 * row_tap + col_tap],
                window,
                preferred_element_type=jnp.float32,
            )
    return total


def transposed(values, weight, row_count, col_count):
    total = jnp.zeros((3, row_count, weight.shape[2], col_count), jnp.float32)
    for row_tap in range(3):
        for col_tap in range(3):
            window = values[
                :, 2 - row_tap : 2 - row_tap + row_count, :, 2 - col_tap : 2 - col_tap + col_count
            ]
            total = total + jnp.einsum(
                "oc,kioj->kicj",
                weight[3 * row_tap + col_tap],
                window,
                preferred_element_type=jnp.float32,
            )
    return total


def on_device(planes, cotangent, conv_weight, context_gain, step_index):
    row_count = planes.shape[1]
    local_channels = planes.shape[2]
    col_count = planes.shape[3]
    side_cells = row_count * lax.axis_size("band")
    first_row = lax.axis_index("band") * row_count
    whole = lax.all_gather(planes, "pc", axis=2, tiled=True)
    gathered = with_halo(whole, (("band", 1),), 1)
    padded = jnp.pad(gathered, ((0, 0), (0, 0), (0, 0), (1, 1)))
    inputs = planes.astype(jnp.float32)
    gain_vec = context_gain.astype(jnp.float32)[None, None, :, None]
    channel_ids = lax.axis_index("pc") * local_channels + jnp.arange(
        local_channels, dtype=jnp.int32
    )
    time_vec = time_embed(step_index, channel_ids, C)[None, None, :, None]
    pre_act = (
        convolve(padded, conv_weight, row_count, col_count)
        + gain_vec * context(inputs, first_row, side_cells)
        + time_vec
    )
    block_out = (inputs + jax.nn.silu(pre_act)).astype(jnp.bfloat16)
    sigma_z = jax.nn.sigmoid(pre_act)
    grad_z = (cotangent.astype(jnp.float32) * sigma_z * (1.0 + pre_act * (1.0 - sigma_z))).astype(
        jnp.bfloat16
    )
    grad_rim = with_halo(grad_z, (("band", 1),), 1)
    grad_rim = jnp.pad(grad_rim, ((0, 0), (0, 0), (0, 0), (1, 1)))
    all_grads, all_weights = (
        lax.all_gather(grad_rim, "pc", axis=2, tiled=True),
        lax.all_gather(conv_weight, "pc", axis=1, tiled=True),
    )
    own_weights = lax.dynamic_slice_in_dim(
        all_weights, lax.axis_index("pc") * local_channels, local_channels, 2
    )
    conv_back = transposed(all_grads, own_weights, row_count, col_count)
    context_back = context(gain_vec * grad_z.astype(jnp.float32), first_row, side_cells)
    input_grad = (cotangent.astype(jnp.float32) + conv_back + context_back).astype(jnp.bfloat16)
    weight_terms = []
    for row_tap in range(3):
        for col_tap in range(3):
            window = padded[:, row_tap : row_tap + row_count, :, col_tap : col_tap + col_count]
            weight_terms.append(
                jnp.einsum("kioj,kicj->oc", grad_z, window, preferred_element_type=jnp.float32)
            )
    weight_grad = lax.psum_scatter(jnp.stack(weight_terms), "band", scatter_dimension=2, tiled=True)
    return (block_out, input_grad, weight_grad)


def solution(mesh):
    in_specs = (
        P(None, "band", "pc", None),
        P(None, "band", "pc", None),
        P(None, "pc", None),
        P("pc"),
        P(),
    )
    out_specs = (P(None, "band", "pc", None), P(None, "band", "pc", None), P(None, "pc", "band"))
    return jax.shard_map(
        on_device, mesh=mesh, in_specs=in_specs, out_specs=out_specs, check_vma=False
    )
```

profile of v0, /device:TPU:4, one launch (start us, length us, event | category | flops | bytes accessed | tf_op | source)
XLA Modules:
  0.0 1482.2 jit_solution(5976371227544056289)
XLA Ops:
  8.1 1.9 convert_reduce_fusion.1
  10.0 0.5 all-gather.6.cloned.1.call-update
  10.6 159.6 %all-gather = f32[1,256,64]{2,0,1:T(1,128)S(1)} all-gather(f32[1,4,64]{2,0,1:T(1,128)S(1)} %bitcast.261), channel_id=2, replica_groups=mesh['band'=64,'pc'=4] {'band'}, dimensions={1}, use_global_device_ids=true | all-gather | bytes 66560 | tf_op jit(solution)/shard_map/all_gather | solution.py:36
  170.2 0.1 copy.82
  171.0 0.7 convert_element_type.40
  171.7 385.7 %all-reduce.5.cloned.1.call-done = f32[3,64,256]{2,1,0:T(8,128)} async-done(((f32[3,64,256]{2,1,0:T(8,128)}), f32[3,64,256]{2,1,0:T(8,128)}) %all-reduce.5.cloned.1.call-update) | async-done | bytes 196624 | tf_op jit(solution)/shard_map/psum | solution.py:35
  557.4 0.9 slice_bitcast_fusion.3
  558.3 0.1 constant_dynamic-slice_fusion.1
  558.5 0.1 broadcast_add_fusion.3
  558.7 1.3 fusion.203
  560.0 1.3 collective-permute-start
  561.3 1.3 collective-permute-start.1
  562.6 0.1 broadcast_add_fusion.4
  562.7 0.4 fusion.159
  563.1 3.4 collective-permute-done
  566.6 4.5 collective-permute-done.1
  571.1 2.4 fusion.5
  573.5 0.4 fusion.161
  573.8 0.7 fusion.163
  574.5 0.7 fusion.152
  575.2 0.4 fusion.156
  575.6 2.9 fusion.202
  578.5 0.3 pad_maximum_fusion.1
  578.8 0.4 fusion.165
  579.2 0.4 fusion.154
  579.6 0.5 fusion.81
  580.1 0.5 copy-done.2
  580.6 0.1 copy-done.4
  580.7 2.6 fusion.151
  583.3 0.6 fusion.91
  583.9 0.6 fusion.97
  584.5 0.6 fusion.103
  585.1 0.6 fusion.109
  585.7 0.6 fusion.115
  586.3 0.6 fusion.121
  586.9 0.6 fusion.127
  587.5 0.6 fusion.133
  588.1 0.6 fusion.139
  588.7 2.5 copy.106
  591.3 0.5 all-gather.10.cloned.1.call-update
  591.9 2.9 collective-permute-start.2
  594.8 1.3 collective-permute-start.3
  596.1 0.9 collective-permute-done.2
  597.0 4.4 collective-permute-done.3
  601.4 1.4 fusion.146
  602.8 156.1 %all-gather.1 = f32[1,256,64]{2,0,1:T(1,128)S(1)} all-gather(f32[1,4,64]{2,0,1:T(1,128)S(1)} %bitcast.262), channel_id=3, replica_groups=mesh['band'=64,'pc'=4] {'band'}, dimensions={1}, use_global_device_ids=true | all-gather | bytes 66560 | tf_op jit(solution)/shard_map/all_gather | solution.py:36
  758.9 0.1 copy.86
  759.0 0.1 broadcast_add_fusion.2
  759.1 379.7 %all-reduce.7.cloned.1.call-done = f32[3,64,256]{2,1,0:T(8,128)} async-done(((f32[3,64,256]{2,1,0:T(8,128)}), f32[3,64,256]{2,1,0:T(8,128)}) %all-reduce.7.cloned.1.call-update) | async-done | bytes 196624 | tf_op jit(solution)/shard_map/psum | solution.py:35
  1138.8 0.9 slice_bitcast_fusion.1
  1139.8 0.1 constant_dynamic-slice_fusion
  1139.9 0.1 broadcast_add_fusion.1
  1140.0 0.1 broadcast_add_fusion
  1140.1 317.1 %reduce-scatter.2.cloned.1.call-done = f32[9,64,4]{1,0,2:T(8,128)} async-done(((f32[9,64,256]{1,0,2:T(8,128)}), f32[9,64,4]{1,0,2:T(8,128)}) %reduce-scatter.2.cloned.1.call-update) | async-done | bytes 9232 | tf_op jit(solution)/shard_map/reduce_scatter | solution.py:124
  1457.2 1.4 copy.107
  1458.6 2.6 fusion.11
  1461.2 1.9 fusion.13
  1463.1 1.6 fusion.15
  1464.7 1.6 fusion.17
  1466.3 1.3 fusion.19
  1467.7 1.6 fusion.21
  1469.3 1.6 fusion.9
  1470.9 1.3 fusion.7
  1472.2 2.6 fusion.85
  (29 shorter events, 0.6 us)
Async XLA Ops:
  8.0 163.7 %copy-start.5 = (bf16[64]{0:T(256)(128)(2,1)S(1)}, bf16[64]{0:T(256)(128)(2,1)}, u32[]{:S(2)}) copy-start(bf16[64]{0:T(256)(128)(2,1)} %param.8) | copy-start | bytes 388
  8.0 549.4 %all-reduce.5.cloned.1.call-start = ((), (), s32[]{:S(2)}) async-start(), calls=%async_computation.2 | async-start | bytes 393216 | tf_op jit(solution)/shard_map/psum | solution.py:35
  9.9 548.7 %all-gather.6.cloned.1.call-start = ((), (), s32[]{:S(2)}) async-start(), calls=%async_computation.1 | async-start | bytes 1966080 | tf_op jit(solution)/shard_map/all_gather | solution.py:86
  10.5 1128.3 %all-reduce.7.cloned.1.call-start = ((), (), s32[]{:S(2)}) async-start(), calls=%async_computation.5 | async-start | bytes 393216 | tf_op jit(solution)/shard_map/psum | solution.py:35
  170.3 392.4 %copy-start.3 = (bf16[9,64,256]{2,1,0:T(8,128)(2,1)S(1)}, bf16[9,64,256]{2,1,0:T(8,128)(2,1)}, u32[]{:S(2)}) copy-start(bf16[9,64,256]{2,1,0:T(8,128)(2,1)} %param.7) | copy-start | bytes 884740
  558.7 4.0 copy-start.1
  560.0 6.6 collective-permute-start
  561.3 9.7 collective-permute-start.1
  579.6 1.0 copy-start.2
  579.6 1.1 copy-start.4
  588.1 869.1 %reduce-scatter.2.cloned.1.call-start = ((), (), s32[]{:S(2)}) async-start(), calls=%async_computation.6 | async-start | bytes 2129920 | tf_op jit(solution)/shard_map/reduce_scatter | solution.py:124
  591.2 867.4 %all-gather.10.cloned.1.call-start = ((), (), s32[]{:S(2)}) async-start(), calls=%async_computation.4 | async-start | bytes 1474560 | tf_op jit(solution)/shard_map/all_gather | solution.py:109
  591.8 866.8 %all-gather.8.cloned.1.call-start = ((), (), s32[]{:S(2)}) async-start(), calls=%async_computation.3 | async-start | bytes 4423680 | tf_op jit(solution)/shard_map/all_gather | solution.py:108
  591.9 5.1 collective-permute-start.2
  594.8 6.6 collective-permute-start.3
  1458.6 4.5 copy-start
Sparse Core Ops, SparseCore 0:
  12.0 545.3 all-reduce.4
  588.2 550.5 all-reduce.6
  1141.3 315.8 reduce-scatter.1
Sparse Core Ops, SparseCore 1:
  12.4 26.7 all-gather.5
  593.6 25.2 all-gather.9
  620.8 37.0 all-gather.7
where the time goes:
time: 1480 us
  waiting for transfers between devices  1100 us (74%)
  blocking collectives  316 us (21%)
  matrix products  27.9 us (2%)
  between operations  16.4 us (1%)
    psum x2, waiting for transfers between devices, pooled(): totals = lax.psum(col_sums, 'band')  765 us
    reduce_scatter x1, waiting for transfers between devices, on_device(): lax.psum_scatter(jnp.stack(weight_terms), 'band', scatter_dimension=2, ti...  317 us
    all_gather x2, blocking collectives, pooled(): row_sums_all = lax.all_gather(row_sums[2], 'band', axis=0, tiled=True)  316 us
  transfers between devices with their start and end apart: 10, of which 7 were waited for; matrix products, arithmetic and copies ran while one was open for 1% of the time, Pallas kernels for 0%

commit v1 on v0

--- a/solution.py
+++ b/solution.py
@@ -32,7 +32,7 @@
 def pooled(values):
     col_sums = jnp.sum(values, axis=1)
     row_sums = jnp.sum(values, axis=3)
-    totals = lax.psum(col_sums, "band")
+    totals = jnp.sum(lax.all_gather(col_sums, "band"), axis=0)
     row_sums_all = lax.all_gather(row_sums[2], "band", axis=0, tiled=True)
     return (totals, row_sums, row_sums_all)
 

time: 1480 us -> 1120 us (0.76)
  waiting for transfers between devices: 1100 us -> 685 us
  other arithmetic: 7.15 us -> 25.5 us
  matrix products: 27.9 us -> 43.5 us
    psum x2 -> x0, waiting for transfers between devices: 765 us -> none  [pooled(): totals = lax.psum(col_sums, 'band')]
    all_gather x0 -> x2, waiting for transfers between devices: none -> 448 us  [pooled(): totals = jnp.sum(lax.all_gather(col_sums, 'band'), axis=0)]
    reduce_scatter x1, waiting for transfers between devices: 317 us -> 147 us  [on_device(): lax.psum_scatter(jnp.stack(weight_terms), 'band', scatter_dimension=2, ti...]
    all_gather x1, waiting for transfers between devices: 0.01 us -> 38.7 us  [on_device(): lax.all_gather(grad_rim, 'pc', axis=2, tiled=True)]
    all_gather x1, waiting for transfers between devices: 0.03 us -> 25.8 us  [on_device(): whole = lax.all_gather(planes, 'pc', axis=2, tiled=True)]
    all_gather x1, waiting for transfers between devices: 0.01 us -> 18.7 us  [on_device(): lax.all_gather(conv_weight, 'pc', axis=1, tiled=True)]
  transfers between devices with their start and end apart: 10 -> 10, of which waited for: 7 -> 8; matrix products, arithmetic and copies ran while one was open for 1% -> 4% of each run, Pallas kernels for 0% -> 0%
where the time goes in v1:
time: 1120 us
  waiting for transfers between devices  685 us (61%)
  blocking collectives  313 us (28%)
  matrix products  43.5 us (4%)
  other arithmetic  25.5 us (2%)
  local copies, waits for them, and re-layouts  24 us (2%)
  between operations  15.1 us (1%)
    all_gather x2, waiting for transfers between devices, pooled(): totals = jnp.sum(lax.all_gather(col_sums, 'band'), axis=0)  448 us
    all_gather x2, blocking collectives, pooled(): row_sums_all = lax.all_gather(row_sums[2], 'band', axis=0, tiled=True)  313 us
    reduce_scatter x1, waiting for transfers between devices, on_device(): lax.psum_scatter(jnp.stack(weight_terms), 'band', scatter_dimension=2, ti...  147 us
    all_gather x1, waiting for transfers between devices, on_device(): lax.all_gather(grad_rim, 'pc', axis=2, tiled=True)  38.7 us
    all_gather x1, waiting for transfers between devices, on_device(): whole = lax.all_gather(planes, 'pc', axis=2, tiled=True)  25.8 us
    dot_general x9, matrix products, transposed(): jnp.einsum('oc,kioj->kicj', weight[3 * row_tap + col_tap], window, prefer...  25.3 us
  transfers between devices with their start and end apart: 10, of which 8 were waited for; matrix products, arithmetic and copies ran while one was open for 4% of the time, Pallas kernels for 0%

profile of v1, /device:TPU:4, one launch (start us, length us, event | category | flops | bytes accessed | tf_op | source)
XLA Modules:
  0.0 1115.7 jit_solution(14229017320800293305)
XLA Ops:
  7.2 0.7 all-gather.10.cloned.1.call-update
  8.0 1.9 convert_reduce_fusion.1
  10.6 25.8 %all-gather.10.cloned.1.call-done = bf16[3,4,256,256]{3,2,1,0:T(8,128)(2,1)} async-done(((bf16[3,4,64,256]{3,2,1,0:T(8,128)(2,1)}), bf16[3,4,256,256]{3,2,1,0:T(8,128)(2,1)}) %all-gather.10.cloned.1.call-update) | async-done | bytes 1572880 | tf_op jit(solution)/shard_map/all_gather | solution.py:86
  36.4 1.3 fusion.203
  37.7 3.7 collective-permute-start
  41.3 1.3 collective-permute-start.1
  42.6 0.7 compare_select_fusion
  43.8 158.7 %all-gather = f32[1,256,64]{2,0,1:T(1,128)S(1)} all-gather(f32[1,4,64]{2,0,1:T(1,128)S(1)} %bitcast.265), channel_id=2, replica_groups=mesh['band'=64,'pc'=4] {'band'}, dimensions={1}, use_global_device_ids=true | all-gather | bytes 66560 | tf_op jit(solution)/shard_map/all_gather | solution.py:36
  202.5 0.7 copy.84
  203.2 1.1 fusion.159
  204.4 0.7 copy-done.14
  205.1 0.7 copy-done.15
  206.2 4.0 fusion.5
  210.6 0.7 fusion.163
  211.3 1.6 fusion.152
  212.8 1.3 fusion.156
  214.5 1.3 fusion.154
  215.8 1.4 fusion.81
  217.2 5.1 fusion.202
  222.3 141.5 %all-gather.16.cloned.1.call-done = f32[192,64,256]{2,1,0:T(8,128)} async-done(((f32[3,64,256]{2,1,0:T(8,128)}), f32[192,64,256]{2,1,0:T(8,128)}) %all-gather.16.cloned.1.call-update) | async-done | bytes 12582928 | tf_op jit(solution)/shard_map/all_gather | solution.py:35
  363.8 6.1 reduce_sum.56
  369.9 1.6 slice_bitcast_fusion.3
  371.4 0.7 constant_dynamic-slice_fusion.1
  372.1 0.8 copy.85
  373.0 0.9 broadcast_add_fusion.4
  373.9 1.0 broadcast_add_fusion.3
  374.9 4.8 fusion.151
  380.3 1.0 copy-done.7
  381.9 0.8 copy-done.12
  384.0 0.7 copy-done.3
  384.7 0.6 fusion.115
  385.3 0.8 copy-done.10
  386.1 0.6 fusion.121
  387.4 0.7 copy-done.5
  388.1 0.6 fusion.133
  388.7 0.8 copy-done.8
  390.1 2.5 copy.108
  393.6 2.5 collective-permute-start.2
  396.1 1.3 collective-permute-start.3
  397.4 0.9 collective-permute-done.2
  398.3 4.3 collective-permute-done.3
  402.7 1.4 fusion.146
  404.6 154.5 %all-gather.2 = f32[1,256,64]{2,0,1:T(1,128)S(1)} all-gather(f32[1,4,64]{2,0,1:T(1,128)S(1)} %bitcast.266), channel_id=4, replica_groups=mesh['band'=64,'pc'=4] {'band'}, dimensions={1}, use_global_device_ids=true | all-gather | bytes 66560 | tf_op jit(solution)/shard_map/all_gather | solution.py:36
  559.3 0.8 broadcast_add_fusion.2
  560.1 147.5 %reduce-scatter.2.cloned.1.call-done = f32[9,64,4]{1,0,2:T(8,128)} async-done(((f32[9,64,256]{1,0,2:T(8,128)}), f32[9,64,4]{1,0,2:T(8,128)}) %reduce-scatter.2.cloned.1.call-update) | async-done | bytes 9232 | tf_op jit(solution)/shard_map/reduce_scatter | solution.py:124
  707.5 1.4 copy.109
  708.9 18.7 %all-gather.14.cloned.1.call-done = bf16[9,256,256]{2,1,0:T(8,128)(2,1)} async-done(((bf16[9,64,256]{2,1,0:T(8,128)(2,1)}), bf16[9,256,256]{2,1,0:T(8,128)(2,1)}) %all-gather.14.cloned.1.call-update) | async-done | bytes 1179664 | tf_op jit(solution)/shard_map/all_gather | solution.py:109
  727.6 38.7 %all-gather.12.cloned.1.call-done = bf16[3,6,256,258]{3,2,1,0:T(8,128)(2,1)} async-done(((bf16[3,6,64,258]{3,2,1,0:T(8,128)(2,1)}), bf16[3,6,256,258]{3,2,1,0:T(8,128)(2,1)}) %all-gather.12.cloned.1.call-update) | async-done | bytes 2377744 | tf_op jit(solution)/shard_map/all_gather | solution.py:108
  766.2 3.5 fusion.11
  769.7 2.8 fusion.13
  772.5 2.5 fusion.15
  775.0 2.5 fusion.17
  777.5 2.2 fusion.19
  779.7 2.5 fusion.21
  782.1 2.5 fusion.9
  784.6 2.2 fusion.7
  786.9 306.2 %all-gather.18.cloned.1.call-done = f32[192,64,256]{2,1,0:T(8,128)} async-done(((f32[3,64,256]{2,1,0:T(8,128)}), f32[192,64,256]{2,1,0:T(8,128)}) %all-gather.18.cloned.1.call-update) | async-done | bytes 12582928 | tf_op jit(solution)/shard_map/all_gather | solution.py:35
  1093.1 6.1 reduce_sum.59
  1099.2 1.6 slice_bitcast_fusion.1
  1100.7 0.7 constant_dynamic-slice_fusion
  1101.4 0.8 copy.89
  1102.3 0.9 broadcast_add_fusion.1
  1103.2 0.9 broadcast_add_fusion
  1104.2 4.7 fusion.85
  (59 shorter events, 7.2 us)
Async XLA Ops:
  7.2 35.5 %copy-start.19 = (bf16[64]{0:T(256)(128)(2,1)S(1)}, bf16[64]{0:T(256)(128)(2,1)}, u32[]{:S(2)}) copy-start(bf16[64]{0:T(256)(128)(2,1)} %param.8) | copy-start | bytes 388
  7.2 29.2 %all-gather.10.cloned.1.call-start = ((), (), s32[]{:S(2)}) async-start(), calls=%async_computation.1 | async-start | bytes 1966080 | tf_op jit(solution)/shard_map/all_gather | solution.py:86
  7.9 355.9 %all-gather.16.cloned.1.call-start = ((), (), s32[]{:S(2)}) async-start(), calls=%async_computation.5 | async-start | bytes 12779520 | tf_op jit(solution)/shard_map/all_gather | solution.py:35
  9.8 697.7 %reduce-scatter.2.cloned.1.call-start = ((), (), s32[]{:S(2)}) async-start(), calls=%async_computation.4 | async-start | bytes 2129920 | tf_op jit(solution)/shard_map/reduce_scatter | solution.py:124
  36.4 166.8 %copy-start.1 = (bf16[3,4,256,256]{3,2,1,0:T(8,128)(2,1)S(1)}, bf16[3,4,256,256]{3,2,1,0:T(8,128)(2,1)}, u32[]{:S(2)}) copy-start(bf16[3,4,256,256]{3,2,1,0:T(8,128)(2,1)} %all-gather.10.cloned.1.call-done) | copy-start | bytes 4718596
  37.7 166.7 %collective-permute-start = (bf16[3,1,256,256]{3,2,1,0:T(8,128)(2,1)S(1)}, bf16[3,1,256,256]{3,2,1,0:T(8,128)(2,1)S(1)}, u32[]{:S(2)}, u32[]{:S(2)}) collective-permute-start(bf16[3,1,256,256]{3,2,1,0:T(8,128)(2,1)S(1)} %get-tuple-element.28), channel_id=1, source_target_pairs={{0,4},{4,8},{8,12},{12,16},{16,20},{20,24},{24,28},{28,32},{32,36}... | collective-permute-start | bytes 1179656 | tf_op jit(solution)/shard_map/ppermute | solution.py:15
  41.3 163.0 %collective-permute-start.1 = (bf16[3,1,256,256]{3,2,1,0:T(8,128)(2,1)S(1)}, bf16[3,1,256,256]{3,2,1,0:T(8,128)(2,1)S(1)}, u32[]{:S(2)}, u32[]{:S(2)}) collective-permute-start(bf16[3,1,256,256]{3,2,1,0:T(8,128)(2,1)S(1)} %get-tuple-element.29), channel_id=1, source_target_pairs={{4,0},{8,4},{12,8},{16,12},{20,16},{24,20},{28,24},{32,28},{36,32}... | collective-permute-start | bytes 1179656 | tf_op jit(solution)/shard_map/ppermute | solution.py:18
  204.3 1.8 copy-start.2
  204.3 0.7 copy-start.14
  205.1 0.7 copy-start.15
  206.1 8.0 copy-start.6
  206.1 8.4 copy-start.4
  206.1 4.0 copy-start.16
  374.9 4.8 copy-start.13
  379.7 9.0 copy-start.17
  379.7 1.5 copy-start.7
  381.3 1.4 copy-start.12
  381.9 1.5 copy-start.11
  383.3 1.4 copy-start.3
  384.7 1.4 copy-start.10
  385.3 1.5 copy-start.9
  386.7 1.4 copy-start.5
  388.1 1.4 copy-start.8
  392.6 1.0 copy-start.18
  392.6 334.9 %all-gather.14.cloned.1.call-start = ((), (), s32[]{:S(2)}) async-start(), calls=%async_computation.3 | async-start | bytes 1474560 | tf_op jit(solution)/shard_map/all_gather | solution.py:109
  393.2 373.0 %all-gather.12.cloned.1.call-start = ((), (), s32[]{:S(2)}) async-start(), calls=%async_computation.2 | async-start | bytes 4423680 | tf_op jit(solution)/shard_map/all_gather | solution.py:108
  393.6 4.7 collective-permute-start.2
  396.1 6.5 collective-permute-start.3
  404.1 689.0 %all-gather.18.cloned.1.call-start = ((), (), s32[]{:S(2)}) async-start(), calls=%async_computation.6 | async-start | bytes 12779520 | tf_op jit(solution)/shard_map/all_gather | solution.py:35
  766.2 6.3 copy-start
Sparse Core Ops, SparseCore 0:
  9.8 26.4 all-gather.9
  38.1 325.5 all-gather.15
  392.8 314.7 reduce-scatter.1
  709.3 18.1 all-gather.13
  729.4 36.8 all-gather.11
  768.0 325.0 all-gather.17
